TPU v7x, 1024 devices: a whole 4x4x32 slice. The times are simulated.
1024 devices in a mesh: rows: 128 (over z, x), rep: 8 (over y, core).
Axes of the slice: x: 4, y: 4, z: 32, core: 2. Of those that a mesh axis runs over, the one named last changes fastest.
Arguments:
- features: bfloat16 [262144, 1024], P('rows', 'rep'), may hold values from -6 to 6
- tile_rows: int32 [128, 4, 16], P('rows'), may hold values from 0 to 15
- tile_cols: int32 [128, 4, 16], P('rows'), may hold values from 0 to 15
- tile_counts: int32 [128, 4], P('rows'), may hold values from 1 to 16, as said below
- tile_values: bfloat16 [128, 4, 16, 128, 128], P('rows'), may hold values from 0 to 0.099609375
- weight: bfloat16 [1024, 1024], P(None, 'rep'), may hold values from -0.1875 to 0.1875
Outputs:
- activated: bfloat16 [262144, 1024], P(('rows', 'rep'))
Inputs may be any that keep to these rules, and one draw needn't show every extreme that they name: `tile_counts`: some row group has all 16 slots live for some owner in every draw.
All inputs are finite; a program needn't handle non-finite values.
Results may differ from a plain program's by a relative error of at most 0.0049.
Values may be sent and summed in bfloat16 or wider, within the bound.
A program may use at most 32 MiB of HBM per device.

v0:
```python
import jax
import jax.numpy as jnp
from jax import lax
from jax.sharding import PartitionSpec as P


def broadcast(block, axis, holder):
    block = jnp.where(lax.axis_index(axis) == holder, block, jnp.zeros_like(block))
    return lax.psum(block, axis)


def shards(features, tile_rows, tile_cols, tile_counts, tile_values, weight):
    owners = lax.axis_size("rows")
    height, width = features.shape
    edge = tile_values.shape[3]
    row_tiles = height // edge
    sections = tile_rows.shape[1]
    slots = tile_rows.shape[2]
    places = jnp.arange(row_tiles, dtype=jnp.int32)
    slot_ids = jnp.arange(slots, dtype=jnp.int32)
    total = jnp.zeros((row_tiles, edge, width), jnp.float32)
    for section in range(sections):
        panel = broadcast(features, "rows", section * (owners // sections))
        blocks = panel.reshape(row_tiles, edge, width)
        picked = jnp.take(blocks, tile_cols[0, section], axis=0)
        products = jnp.einsum(
            "sij,sjk->sik", tile_values[0, section], picked, preferred_element_type=jnp.float32
        )
        live = slot_ids < tile_counts[0, section]
        placing = ((tile_rows[0, section][None, :] == places[:, None]) & live[None, :]).astype(
            jnp.float32
        )
        total = total + jnp.einsum(
            "ts,sik->tik", placing, products, precision=lax.Precision.HIGHEST
        )
    aggregate = total.reshape(height, width).astype(jnp.bfloat16)
    mixed = jnp.dot(
        lax.all_gather(aggregate, "rep", axis=1, tiled=True),
        weight,
        preferred_element_type=jnp.float32,
    )
    activated = jnp.maximum(mixed, 0.0).astype(jnp.bfloat16)
    return lax.all_to_all(activated, "rep", split_axis=0, concat_axis=1, tiled=True)


def solution(mesh):
    return jax.shard_map(
        shards,
        mesh=mesh,
        in_specs=(
            P("rows", "rep"),
            P("rows", None, None),
            P("rows", None, None),
            P("rows", None),
            P("rows", None, None, None, None),
            P(None, "rep"),
        ),
        out_specs=P(("rows", "rep"), None),
        check_vma=False,
    )
```

profile of v0, /device:TPU:1, one launch (start us, length us, event | category | flops | bytes accessed | tf_op | source)
XLA Modules:
  0.0 627.5 jit_solution(16693735521836345911)
XLA Ops:
  6.5 0.0 copy-start
  6.5 0.0 all-reduce.3.cloned.1.call-start
  6.5 0.0 copy-start.5
  6.5 0.0 copy-start.6
  6.5 0.0 copy-start.7
  6.6 2.4 broadcast_select_fusion
  9.0 0.0 all-reduce.3.cloned.1.call-update
  9.0 0.0 all-gather.2.cloned.1.call-start
  9.1 0.0 copy-done.5
  9.1 0.7 fusion.55
  9.7 0.7 iota_compare_fusion.7
  10.4 0.6 iota_compare_fusion.6
  11.1 0.6 iota_compare_fusion.5
  11.7 0.6 iota_compare_fusion.4
  12.3 0.0 copy-done.6
  12.3 0.0 copy-done.7
  12.3 506.5 %all-reduce.3.cloned.1.call-done = (bf16[16,128,128]{2,1,0:T(8,128)(2,1)}, bf16[16,128,128]{2,1,0:T(8,128)(2,1)}, bf16[16,128,128]{2,1,0:T(8,128)(2,1)}, bf16[16,128,128]{2,1,0:T(8,128)(2,1)}) async-done(((bf16[16,128,128]{2,1,0:T(8,128)(2,1)}, bf16[16,128,128]{2,1,0:T(8,128)(2,1)}, bf16[16,128,128]{2,1,0:T(8,128)(2,1)}, bf16[16,128,128]{2,1,0:T(8,128)(2,1)}), (bf16[16,128,128]{2,1,0:T(8,128)(2,1)}, ...) | async-done | bytes 2097168 | tf_op jit(solution)/shard_map/psum | solution.py:9
  518.9 1.7 gather_fusion
  520.6 0.0 copy-start.4
  520.6 1.8 fusion.13
  522.3 1.4 copy.10
  523.7 0.0 copy-done.4
  523.7 0.6 gather_fusion.1
  524.4 0.0 copy-start.3
  524.4 1.8 fusion.11
  526.2 0.5 copy.11
  526.7 0.0 copy-done.3
  526.7 0.6 gather_fusion.2
  527.4 0.0 copy-start.2
  527.4 1.8 fusion.9
  529.2 1.4 copy.12
  530.6 0.0 copy-done.2
  530.6 0.6 gather_fusion.3
  531.2 1.7 fusion.7
  533.0 0.5 copy.13
  533.5 1.8 fusion.5
  535.3 0.0 copy-start.1
  535.3 0.6 convolution_add_fusion.2
  535.9 0.6 copy-done.1
  536.5 0.6 convolution_add_fusion.1
  537.2 0.6 fusion.1
  537.8 0.9 copy.8
  538.7 0.0 all-gather.2.cloned.1.call-update
  538.8 64.2 %all-gather.2.cloned.1.call-done = bf16[2048,1024]{1,0:T(8,128)(2,1)} async-done(((bf16[2048,128]{1,0:T(8,128)(2,1)}), bf16[2048,1024]{1,0:T(8,128)(2,1)}) %all-gather.2.cloned.1.call-update) | async-done | bytes 4194320 | tf_op jit(solution)/shard_map/all_gather | solution.py:38
  603.0 0.0 copy-done
  603.0 3.4 fusion
  606.4 13.4 %all_to_all.19 = bf16[8,256,128]{2,1,0:T(8,128)(2,1)S(1)} all-to-all(bf16[8,256,128]{2,1,0:T(8,128)(2,1)S(1)} %bitcast.79), channel_id=1, replica_groups=mesh['rows'=128,'rep'=8] {'rep'}, dimensions={0} | all-to-all | bytes 1048576 | tf_op jit(solution)/shard_map/all_to_all | solution.py:43
  619.8 0.9 copy_bitcast_fusion
  (4 shorter events, 0.0 us)
Async XLA Ops:
  6.5 596.5 %copy-start = (bf16[1024,128]{1,0:T(8,128)(2,1)S(1)}, bf16[1024,128]{1,0:T(8,128)(2,1)}, u32[]{:S(2)}) copy-start(bf16[1024,128]{1,0:T(8,128)(2,1)} %param.13) | copy-start | bytes 786436
  6.5 512.3 %all-reduce.3.cloned.1.call-start = ((), (), s32[]{:S(2)}) async-start(), calls=%async_computation.2 | async-start | bytes 4194304 | tf_op jit(solution)/shard_map/psum | solution.py:9
  6.5 2.5 copy-start.5
  6.5 5.7 copy-start.6
  6.5 5.8 copy-start.7
  9.0 594.0 %all-gather.2.cloned.1.call-start = ((), (), s32[]{:S(2)}) async-start(), calls=%async_computation.1 | async-start | bytes 4718592 | tf_op jit(solution)/shard_map/all_gather | solution.py:38
  520.6 3.2 copy-start.4
  524.4 2.3 copy-start.3
  527.4 3.2 copy-start.2
  535.3 1.2 copy-start.1
Sparse Core Ops, SparseCore 0:
  11.0 507.7 all-reduce.2
  538.9 64.0 all-gather.1
where the time goes:
time: 628 us
  waiting for transfers between devices  571 us (91%)
  matrix products  14.2 us (2%)
  between operations  13.6 us (2%)
  blocking collectives  13.4 us (2%)
  local copies, waits for them, and re-layouts  10.5 us (2%)
    psum x1, waiting for transfers between devices, broadcast(): return lax.psum(block, axis)  507 us
    all_gather x1, waiting for transfers between devices, shards(): lax.all_gather(aggregate, 'rep', axis=1, tiled=True)  64.2 us
    all_to_all x1, blocking collectives, shards(): lax.all_to_all(activated, 'rep', split_axis=0, concat_axis=1, tiled=True)  13.4 us
  transfers between devices with their start and end apart: 2, of which 2 were waited for; matrix products, arithmetic and copies ran while one was open for 1% of the time, Pallas kernels for 0%

commit v1 on v0

v1 whole, which is shorter than its diff:
```python
import jax
import jax.numpy as jnp
from jax import lax
from jax.experimental import pallas as pl
from jax.experimental.pallas import tpu as pltpu
from jax.sharding import PartitionSpec as P

MESH = pl.DeviceIdType.MESH
ZS, XS, REPS = 32, 4, 8
SECTIONS, SLOTS, TILE = 4, 16, 128
GAP = ZS // SECTIONS
HALF = ZS // 2
GROUP = 4 * TILE


def kernel(
    rows_ref, cols_ref, counts_ref, feat_ref, tiles_ref, weight_ref, out_ref,
    panel, whole, tiles, weights, sums, block_out, block_in, prev, last,
    local_sem, recv_sem, send_sem, wsend_sem, wrecv_sem, bsend_sem, brecv_sem,
):
    me, rep = lax.axis_index("rows"), lax.axis_index("rep")
    z, x = me // XS, me % XS

    def at(dz, dx):
        return (((z + dz + ZS) % ZS) * XS + (x + dx + XS) % XS, rep)

    def other(i):
        return lax.rem(rep + i, REPS)

    is_owner = jnp.logical_and(x == 0, z % GAP == 0)
    mine = z // GAP

    barrier = pltpu.get_barrier_semaphore()
    partners = [at(d, 0) for d in (1, -1, 2, -2, 3, -3, 4, -4)] + [at(0, d) for d in (1, -1, 2)]
    for partner in partners:
        pl.semaphore_signal(barrier, inc=1, device_id=partner, device_id_type=MESH)
    for i in range(1, REPS):
        pl.semaphore_signal(barrier, inc=1, device_id=(me, other(i)), device_id_type=MESH)

    own_panel = pltpu.make_async_copy(feat_ref, panel.at[mine], local_sem.at[0])
    own_weight = pltpu.make_async_copy(weight_ref, weights.at[rep], local_sem.at[1])
    own_tiles = pltpu.make_async_copy(tiles_ref.at[0], tiles, local_sem.at[2])

    @pl.when(is_owner)
    def _():
        own_panel.start()

    own_tiles.start()
    own_weight.start()
    sums[SECTIONS * SLOTS] = jnp.zeros((TILE, TILE), jnp.float32)

    def along(section):
        dz = lax.rem(z - GAP * section + ZS, ZS)
        far = jnp.where(dz <= HALF, dz, ZS - dz)
        return dz, (far + 3) // 4

    for t in range(16):
        last[t] = SECTIONS * SLOTS

    def link(step, carry):
        def of(section, carry):
            _, turn = along(section)

            @pl.when(turn == step)
            def _():
                def slot(j, carry):
                    row = rows_ref[0, section, j]
                    here = section * SLOTS + j
                    prev[here] = last[row]
                    row = jnp.where(j < counts_ref[0, section], row, 16)
                    for t in range(16):
                        last[t] = jnp.where(row == t, here, last[t])
                    return carry

                lax.fori_loop(0, SLOTS, slot, 0)

            return carry

        return lax.fori_loop(0, SECTIONS, of, carry)

    lax.fori_loop(0, 5, link, 0)

    pl.semaphore_wait(barrier, len(partners) + REPS - 1)

    def wcopy(i):
        return pltpu.make_async_remote_copy(
            weight_ref, weights.at[rep], wsend_sem.at[i], wrecv_sem.at[rep],
            device_id=(me, other(i)), device_id_type=MESH)

    def rows_of(section, tile, count=1):
        return panel.at[section, pl.ds(tile, count)]

    def copy(section, tile, count, send, recv, to):
        ref = rows_of(section, tile, count)
        return pltpu.make_async_remote_copy(
            ref, ref, send_sem.at[section, send], recv_sem.at[section, recv], device_id=to, device_id_type=MESH)

    def sends_spread(section, act, wait):
        dz, _ = along(section)
        in_row = dz == 0

        @pl.when(in_row)
        def _():
            for b in range(4):
                @pl.when(x == 0)
                def _():
                    for i, dx in enumerate((2, 1, 3)):
                        act(copy(section, 4 * dx + b, 1, 3 * b + i, b, at(0, dx)))

                if wait:
                    @pl.when(x != 0)
                    def _():
                        copy(section, 4 * x + b, 1, 0, b, at(0, 1)).wait_recv()

                act(copy(section, 4 * x + b, 1, 12 + 2 * b, 0, at(b if b else 4, 0)))
                act(copy(section, 4 * x + b, 1, 13 + 2 * b, 0, at(b - 4, 0)))

        own = 4 * x + z % 4

        @pl.when(jnp.logical_not(in_row))
        def _():
            if wait:
                copy(section, own, 1, 0, 0, at(1, 0)).wait_recv()

            @pl.when(dz + 4 <= HALF)
            def _():
                act(copy(section, own, 1, 12, 0, at(4, 0)))

            @pl.when(dz - 4 > HALF)
            def _():
                act(copy(section, own, 1, 12, 0, at(-4, 0)))

        skip = 2 - 4 * (section % 2)

        @pl.when(dz + 1 != ZS)
        def _():
            act(copy(section, own, 1, 20, 4, at(1, 0)))

        @pl.when(dz != 1)
        def _():
            act(copy(section, own, 1, 21, 5, at(-1, 0)))

        @pl.when(lax.rem(dz + skip + ZS, ZS) != 0)
        def _():
            act(copy(section, own, 1, 22, 6, at(skip, 0)))

    def sends_across(section, act, wait):
        dz, _ = along(section)
        if wait:
            @pl.when(dz != 0)
            def _():
                copy(section, 4 * x + (z + 3) % 4, 1, 0, 4, at(1, 0)).wait_recv()
                copy(section, 4 * x + (z + 1) % 4, 1, 0, 5, at(1, 0)).wait_recv()
                copy(section, 4 * x + (z + 2) % 4, 1, 0, 6, at(1, 0)).wait_recv()

        @pl.when(jnp.logical_or(dz != 0, x != 3))
        def _():
            act(copy(section, 4 * x, 4, 23, 7, at(0, 1)))

        @pl.when(jnp.logical_or(dz != 0, x != 1))
        def _():
            act(copy(section, 4 * x, 4, 24, 8, at(0, -1)))

    def sends_on(section, act, wait):
        dz, _ = along(section)
        left, right = (x + 3) % 4, (x + 1) % 4
        gets = jnp.logical_or(dz != 0, x != 0)
        if wait:
            @pl.when(gets)
            def _():
                copy(section, 4 * left, 4, 0, 7, at(0, 1)).wait_recv()

        @pl.when(jnp.logical_or(dz != 0, x != 3))
        def _():
            act(copy(section, 4 * left, 2, 25, 9, at(0, 1)))

        if wait:
            @pl.when(gets)
            def _():
                copy(section, 4 * right, 4, 0, 8, at(0, 1)).wait_recv()

        @pl.when(jnp.logical_or(dz != 0, x != 1))
        def _():
            act(copy(section, 4 * right + 2, 2, 26, 10, at(0, -1)))

    def products(section):
        dz, _ = along(section)

        @pl.when(jnp.logical_or(dz != 0, x != 0))
        def _():
            facing = (x + 2) % 4
            copy(section, 4 * facing, 2, 0, 9, at(0, 1)).wait_recv()
            copy(section, 4 * facing + 2, 2, 0, 10, at(0, 1)).wait_recv()

        whole[...] = panel[section]
        for j in range(SLOTS):
            here = section * SLOTS + j
            sums[here] = sums[prev[here]] + jnp.dot(
                tiles[section, j], whole[cols_ref[0, section, j]], preferred_element_type=jnp.float32)

    def start(c):
        c.start()

    def step(now, carry):
        def for_each(turn, what):
            def of(section, carry):
                _, first = along(section)

                @pl.when(first == turn)
                def _():
                    what(section)

                return carry

            lax.fori_loop(0, SECTIONS, of, 0)

        for_each(now, lambda s: sends_spread(s, start, True))

        @pl.when(now == 0)
        def _():
            def one(i, carry):
                wcopy(i).start()
                return carry

            lax.fori_loop(1, REPS, one, 0)

        for_each(now - 1, lambda s: sends_across(s, start, True))
        for_each(now - 2, lambda s: sends_on(s, start, True))
        for_each(now - 3, products)
        return carry

    @pl.when(is_owner)
    def _():
        own_panel.wait()

    own_tiles.wait()
    own_weight.wait()
    lax.fori_loop(0, 8, step, 0)

    def bcopy(i):
        to = other(i)
        return pltpu.make_async_remote_copy(
            block_out.at[to], block_in.at[rep], bsend_sem.at[i], brecv_sem.at[rep],
            device_id=(me, to), device_id_type=MESH)

    def send_block(i, carry):
        to = other(i)
        for half in range(2):
            block_out[to, pl.ds(half * TILE, TILE), :] = sums[last[2 * to + half]].astype(jnp.bfloat16)

        bcopy(i).start()
        return carry

    lax.fori_loop(1, REPS, send_block, 0)
    for half in range(2):
        block_in[rep, pl.ds(half * TILE, TILE), :] = sums[last[2 * rep + half]].astype(jnp.bfloat16)

    def arrived(i, carry):
        source = other(i)
        pltpu.make_async_remote_copy(
            weight_ref, weights.at[source], wsend_sem.at[i], wrecv_sem.at[source],
            device_id=(me, source), device_id_type=MESH).wait_recv()
        pltpu.make_async_remote_copy(
            block_out.at[source], block_in.at[source], bsend_sem.at[i], brecv_sem.at[source],
            device_id=(me, source), device_id_type=MESH).wait_recv()
        return carry

    lax.fori_loop(1, REPS, arrived, 0)

    left = jnp.concatenate([block_in[i] for i in range(REPS)], axis=1)
    for q in range(REPS // 2):
        right = jnp.concatenate([weights[2 * q], weights[2 * q + 1]], axis=1)
        mixed = jnp.dot(left, right, preferred_element_type=jnp.float32)
        out_ref[:, pl.ds(2 * q * TILE, 2 * TILE)] = jnp.maximum(mixed, 0.0).astype(jnp.bfloat16)

    def finish(section, carry):
        def done(c):
            c.wait_send()

        sends_spread(section, done, False)
        sends_across(section, done, False)
        sends_on(section, done, False)
        return carry

    lax.fori_loop(0, SECTIONS, finish, 0)

    def sent(i, carry):
        wcopy(i).wait_send()
        bcopy(i).wait_send()
        return carry

    lax.fori_loop(1, REPS, sent, 0)


def shards(features, tile_rows, tile_cols, tile_counts, tile_values, weight):
    height, width = features.shape
    smem = pl.BlockSpec(memory_space=pltpu.SMEM)
    hbm = pl.BlockSpec(memory_space=pl.ANY)
    dma = pltpu.SemaphoreType.DMA
    return pl.pallas_call(
        kernel,
        out_shape=jax.ShapeDtypeStruct((height // REPS, width * REPS), jnp.bfloat16),
        in_specs=[smem, smem, smem, hbm, hbm, hbm],
        out_specs=pl.BlockSpec(memory_space=pltpu.VMEM),
        scratch_shapes=[
            pltpu.VMEM((SECTIONS, 16, TILE, width), jnp.bfloat16),
            pltpu.VMEM((16, TILE, width), jnp.bfloat16),
            pltpu.VMEM((SECTIONS, SLOTS, TILE, TILE), jnp.bfloat16),
            pltpu.VMEM((REPS, weight.shape[0], weight.shape[1]), jnp.bfloat16),
            pltpu.VMEM((SECTIONS * SLOTS + 1, TILE, TILE), jnp.float32),
            pltpu.VMEM((REPS, height // REPS, width), jnp.bfloat16),
            pltpu.VMEM((REPS, height // REPS, width), jnp.bfloat16),
            pltpu.SMEM((SECTIONS * SLOTS,), jnp.int32),
            pltpu.SMEM((16,), jnp.int32),
            dma((3,)),
            dma((SECTIONS, 11)),
            dma((SECTIONS, 27)),
            dma((REPS,)),
            dma((REPS,)),
            dma((REPS,)),
            dma((REPS,)),
        ],
        compiler_params=pltpu.CompilerParams(
            collective_id=0, has_side_effects=True, vmem_limit_bytes=60 << 20
        ),
        cost_estimate=pl.CostEstimate(flops=1_610_612_736, bytes_accessed=8_000_000, transcendentals=0),
        name="layer",
    )(tile_rows, tile_cols, tile_counts, features.reshape(16, TILE, width), tile_values, weight)


def solution(mesh):
    return jax.shard_map(
        shards,
        mesh=mesh,
        in_specs=(
            P("rows", "rep"),
            P("rows", None, None),
            P("rows", None, None),
            P("rows", None),
            P("rows", None, None, None, None),
            P(None, "rep"),
        ),
        out_specs=P(("rows", "rep"), None),
        check_vma=False,
    )
```

time: 628 us -> 75.3 us (0.12)
  waiting for transfers between devices: 571 us -> 0 us
  Pallas kernels: 0 us -> 73.2 us
  matrix products: 14.2 us -> 0 us
  between operations: 13.6 us -> 0.01 us
  blocking collectives: 13.4 us -> 0 us
  local copies, waits for them, and re-layouts: 10.5 us -> 1.87 us
    psum x1 -> x0, waiting for transfers between devices: 507 us -> none  [broadcast(): return lax.psum(block, axis)]
    pallas_call x0 -> x1, Pallas kernels: none -> 73.2 us  [shards(): pl.pallas_call(kernel, out_shape=jax.ShapeDtypeStruct((height // REPS, wi...]
    all_gather x1 -> x0, waiting for transfers between devices: 64.2 us -> none  [shards(): lax.all_gather(aggregate, 'rep', axis=1, tiled=True)]
    dot_general x9 -> x0, matrix products: 14.2 us -> none  [the longest x4 7.08 us: shards(): jnp.einsum('sij,sjk->sik', tile_values[0, section], picked, preferred_ele...]
    all_to_all x1 -> x0, blocking collectives: 13.4 us -> none  [shards(): lax.all_to_all(activated, 'rep', split_axis=0, concat_axis=1, tiled=True)]
  transfers between devices with their start and end apart: 2 -> 0, of which waited for: 2 -> 0; matrix products, arithmetic and copies ran while one was open for 1% -> 0% of each run, Pallas kernels for 0% -> 0%
where the time goes in v1:
time: 75.3 us; the launch traced here: 75.1 us
  Pallas kernels  73.2 us (97%)
  local copies, waits for them, and re-layouts  1.87 us (2%)
    pallas_call x1, Pallas kernels, shards(): pl.pallas_call(kernel, out_shape=jax.ShapeDtypeStruct((height // REPS, wi...  73.2 us
    unnamed x1, local copies, waits for them, and re-layouts  1.87 us

profile of v1, /device:TPU:1, one launch (start us, length us, event | category | flops | bytes accessed | tf_op | source)
XLA Modules:
  0.0 75.1 jit_solution(17372151020127245585)
XLA Ops:
  0.0 73.2 %layer.1 = bf16[256,1024]{1,0:T(8,128)(2,1)} custom-call(s32[1,4,16]{2,1,0:T(4,128)} %rows_ref.1, s32[1,4,16]{2,1,0:T(4,128)} %cols_ref.1, s32[1,4]{1,0:T(1,128)} %counts_ref.1, bf16[16,128,128]{2,1,0:T(8,128)(2,1)} %bitcast.1, bf16[1,4,16,128,128]{4,3,2,1,0:T(8,128)(2,1)} %tiles_ref.1, bf16[1024,128]{1,0:T(8,128)(2,1)} %weight_ref.1), custom_call_target="tpu_custom_call" | custom-call | flops 1610612736 | bytes 8000000 | tf_op jit(solution)/shard_map/layer/pallas_call | solution.py:300
  73.2 1.9 %copy.8 = bf16[256,1024]{1,0:T(8,128)(2,1)} copy(bf16[256,1024]{1,0:T(8,128)(2,1)} %layer.1) | data formatting | bytes 1048576

commit v2 on v1

v2 whole, which is shorter than its diff:
```python
import jax
import jax.numpy as jnp
from jax import lax
from jax.experimental import pallas as pl
from jax.experimental.pallas import tpu as pltpu
from jax.sharding import PartitionSpec as P

MESH = pl.DeviceIdType.MESH
ZS, XS, REPS = 32, 4, 8
SECTIONS, SLOTS, TILE = 4, 16, 128
GAP = ZS // SECTIONS
HALF = ZS // 2
HOP = 4
NONE = SECTIONS * SLOTS
OUT = pltpu.VMEM


def kernel(
    rows_hbm, cols_hbm, counts_hbm, feat_ref, tiles_ref, weight_ref, out_ref,
    panel, whole, tiles, weights, sums, block_out, block_in, rows_ref, cols_ref, counts_ref, prev, last,
    local_sem, recv_sem, send_sem, wsend_sem, wrecv_sem, bsend_sem, brecv_sem,
):
    me, rep = lax.axis_index("rows"), lax.axis_index("rep")
    z, x = me // XS, me % XS
    past = z % GAP

    def at(dz, dx):
        return (((z + dz + ZS) % ZS) * XS + (x + dx + XS) % XS, rep)

    def other(i):
        far, turn = 3 - (i - 1) // 2, 1 - (i - 1) % 2
        return 2 * ((rep // 2 + far) % 4) + (rep + turn) % 2

    is_owner = jnp.logical_and(x == 0, past == 0)

    barrier = pltpu.get_barrier_semaphore()

    def greet(to):
        pl.semaphore_signal(barrier, inc=1, device_id=to, device_id_type=MESH)

    for d in range(HOP, 0, -1):
        greet(at(d, 0))
        greet(at(-d, 0))

    greet(at(0, 1))
    greet(at(0, -1))

    @pl.when(jnp.logical_and(past == 0, x == 2))
    def _():
        greet(at(0, -2))

    for i in range(1, REPS):
        greet((me, other(i)))

    own_panel = pltpu.make_async_copy(feat_ref, panel.at[z // GAP], local_sem.at[0])
    own_weight = pltpu.make_async_copy(weight_ref, weights.at[rep], local_sem.at[1])
    own_tiles = pltpu.make_async_copy(tiles_ref.at[0], tiles, local_sem.at[2])
    lists = [
        pltpu.make_async_copy(rows_hbm, rows_ref, local_sem.at[3]),
        pltpu.make_async_copy(cols_hbm, cols_ref, local_sem.at[4]),
        pltpu.make_async_copy(counts_hbm, counts_ref, local_sem.at[5]),
    ]

    @pl.when(is_owner)
    def _():
        own_panel.start()

    for c in lists + [own_tiles, own_weight]:
        c.start()
    sums[NONE] = jnp.zeros((TILE, TILE), jnp.float32)

    def along(section):
        dz = lax.rem(z - GAP * section + ZS, ZS)
        far = jnp.where(dz <= HALF, dz, ZS - dz)
        return dz, (far + HOP - 1) // HOP

    def make_links():
        for c in lists:
            c.wait()
        keys = [along(s)[1] * SECTIONS + s for s in range(SECTIONS)]
        ranks = [sum((other < key).astype(jnp.int32) for other in keys) for key in keys]
        order = [sum(jnp.where(rank == k, s, 0) for s, rank in enumerate(ranks)) for k in range(SECTIONS)]

        def slot(i, ends):
            k, j = i // SLOTS, i % SLOTS
            section = sum(jnp.where(k == n, s, 0) for n, s in enumerate(order))
            row = jnp.where(j < counts_ref[0, section], rows_ref[0, section, j], 16)
            here = section * SLOTS + j
            before = jnp.int32(NONE)
            after = []
            for t in range(16):
                same = row == t
                before = jnp.where(same, ends[t], before)
                after.append(jnp.where(same, here, ends[t]))
            prev[here] = before
            return tuple(after)

        ends = lax.fori_loop(0, NONE, slot, (jnp.int32(NONE),) * 16)
        for t in range(16):
            last[t] = ends[t]

    def wcopy(i):
        return pltpu.make_async_remote_copy(
            weight_ref, weights.at[rep], wsend_sem.at[i], wrecv_sem.at[rep],
            device_id=(me, other(i)), device_id_type=MESH)

    def copy(section, group, b, send, recv, to, count=1):
        ref = panel.at[section, pl.ds(4 * group + b, count)]
        return pltpu.make_async_remote_copy(
            ref, ref, send_sem.at[section, send], recv_sem.at[section, recv], device_id=to, device_id_type=MESH)

    def gets(section):
        dz, _ = along(section)
        return jnp.logical_or(dz != 0, x != 0)

    def spread(section, act, wait):
        dz, _ = along(section)
        in_row = dz == 0

        @pl.when(in_row)
        def _():
            @pl.when(x == 0)
            def _():
                for b in (0, 3, 1, 2):
                    for i, dx in enumerate((2, 1, 3)):
                        act(copy(section, dx, b, 3 * b + i, b, at(0, dx)))

            needs = {4: (0,), 3: (3, 1), 2: (2,)}
            for d in range(HOP, 0, -1):
                if wait and d in needs:
                    @pl.when(x != 0)
                    def _():
                        for b in needs[d]:
                            copy(section, x, b, 0, b, at(0, 1)).wait_recv()

                act(copy(section, x, d % 4, 10 + 2 * d, 0, at(d, 0)))
                act(copy(section, x, -d % 4, 11 + 2 * d, 0, at(-d, 0)))

        own = z % 4

        @pl.when(jnp.logical_not(in_row))
        def _():
            if wait:
                copy(section, x, own, 0, 0, at(1, 0)).wait_recv()

            @pl.when(dz <= HALF - HOP)
            def _():
                act(copy(section, x, own, 12, 0, at(HOP, 0)))

            @pl.when(dz > HALF + HOP)
            def _():
                act(copy(section, x, own, 12, 0, at(-HOP, 0)))

        out = dz <= HALF
        far = jnp.where(out, dz, ZS - dz)
        place = (far + 3) % 4
        for i in range(1, 4):
            step = (place + i) % 4 - place

            @pl.when(jnp.logical_and(far > 0, jnp.logical_or(out, far + step != HALF)))
            def _():
                act(copy(section, x, own, 27 + i, 4 + own, at(jnp.where(out, step, -step), 0)))

        @pl.when(dz == HALF)
        def _():
            for i in range(1, 4):
                act(copy(section, x, own, 30 + i, 4 + own, at(i, 0)))

    def across(section, act, wait):
        dz, _ = along(section)
        if wait:
            @pl.when(dz != 0)
            def _():
                for step in (1, 2, 3):
                    b = (z + step) % 4
                    copy(section, x, b, 0, 4 + b, at(1, 0)).wait_recv()

        for first, right, left in ((True, 0, 2), (False, 2, 0)):
            @pl.when(jnp.logical_or(dz != 0, x != 3))
            def _():
                act(copy(section, x, right, 34 if first else 38, 8 if first else 12, at(0, 1), 2))

            @pl.when(jnp.logical_or(dz != 0, x != 1))
            def _():
                act(copy(section, x, left, 35 if first else 39, 9 if first else 13, at(0, -1), 2))

    def onward(section, act, wait):
        dz, _ = along(section)
        left, right = (x + 3) % 4, (x + 1) % 4
        if wait:
            @pl.when(gets(section))
            def _():
                copy(section, left, 0, 0, 8, at(0, 1), 2).wait_recv()

        @pl.when(jnp.logical_or(dz != 0, x != 3))
        def _():
            act(copy(section, left, 0, 36, 10, at(0, 1), 2))

        if wait:
            @pl.when(gets(section))
            def _():
                copy(section, right, 2, 0, 9, at(0, 1), 2).wait_recv()

        @pl.when(jnp.logical_or(dz != 0, x != 1))
        def _():
            act(copy(section, right, 2, 37, 11, at(0, -1), 2))

    def complete(section):
        @pl.when(gets(section))
        def _():
            facing = (x + 2) % 4
            copy(section, (x + 3) % 4, 2, 0, 12, at(0, 1), 2).wait_recv()
            copy(section, (x + 1) % 4, 0, 0, 13, at(0, 1), 2).wait_recv()
            copy(section, facing, 0, 0, 10, at(0, 1), 2).wait_recv()
            copy(section, facing, 2, 0, 11, at(0, 1), 2).wait_recv()

    def products(section):
        complete(section)
        whole[...] = panel[section]
        for j in range(SLOTS):
            here = section * SLOTS + j
            sums[here] = sums[prev[here]] + jnp.dot(
                tiles[section, j], whole[cols_ref[0, section, j]], preferred_element_type=jnp.float32)

    def start(c):
        c.start()

    def step(now, carry):
        def for_each(turn, what):
            def of(section, carry):
                _, first = along(section)

                @pl.when(first == turn)
                def _():
                    what(section)

                return carry

            lax.fori_loop(0, SECTIONS, of, 0)

        for_each(now, lambda s: spread(s, start, True))

        @pl.when(now == 0)
        def _():
            def one(i, carry):
                wcopy(i).start()
                return carry

            lax.fori_loop(1, REPS, one, 0)
            make_links()
            own_tiles.wait()

        for_each(now - 1, lambda s: across(s, start, True))
        for_each(now - 2, lambda s: onward(s, start, True))
        for_each(now - 3, products)
        return carry

    pl.semaphore_wait(barrier, jnp.where(is_owner, 18, 17))

    @pl.when(is_owner)
    def _():
        own_panel.wait()

    lax.fori_loop(0, 8, step, 0)

    def bcopy(i):
        to = other(i)
        return pltpu.make_async_remote_copy(
            block_out.at[to], block_in.at[rep], bsend_sem.at[i], brecv_sem.at[rep],
            device_id=(me, to), device_id_type=MESH)

    def send_block(i, carry):
        to = other(i)
        for half in range(2):
            block_out[to, pl.ds(half * TILE, TILE), :] = sums[last[2 * to + half]].astype(jnp.bfloat16)

        bcopy(i).start()
        return carry

    lax.fori_loop(1, REPS, send_block, 0)
    for half in range(2):
        block_in[rep, pl.ds(half * TILE, TILE), :] = sums[last[2 * rep + half]].astype(jnp.bfloat16)

    own_weight.wait()

    def arrived(i, carry):
        source = other(i)
        pltpu.make_async_remote_copy(
            weight_ref, weights.at[source], wsend_sem.at[i], wrecv_sem.at[source],
            device_id=(me, source), device_id_type=MESH).wait_recv()
        pltpu.make_async_remote_copy(
            block_out.at[source], block_in.at[source], bsend_sem.at[i], brecv_sem.at[source],
            device_id=(me, source), device_id_type=MESH).wait_recv()
        return carry

    lax.fori_loop(1, REPS, arrived, 0)

    left = jnp.concatenate([block_in[i] for i in range(REPS)], axis=1)
    for q in range(REPS // 2):
        right = jnp.concatenate([weights[2 * q], weights[2 * q + 1]], axis=1)
        mixed = jnp.dot(left, right, preferred_element_type=jnp.float32)
        out_ref[:, pl.ds(2 * q * TILE, 2 * TILE)] = jnp.maximum(mixed, 0.0).astype(jnp.bfloat16)

    def finish(section, carry):
        def done(c):
            c.wait_send()

        spread(section, done, False)
        across(section, done, False)
        onward(section, done, False)
        return carry

    lax.fori_loop(0, SECTIONS, finish, 0)

    def sent(i, carry):
        wcopy(i).wait_send()
        bcopy(i).wait_send()
        return carry

    lax.fori_loop(1, REPS, sent, 0)


def shards(features, tile_rows, tile_cols, tile_counts, tile_values, weight):
    height, width = features.shape
    hbm = pl.BlockSpec(memory_space=pl.ANY)
    dma = pltpu.SemaphoreType.DMA
    return pl.pallas_call(
        kernel,
        out_shape=OUT((height // REPS, width * REPS), jnp.bfloat16),
        in_specs=[hbm] * 6,
        out_specs=pl.BlockSpec(memory_space=pltpu.VMEM),
        scratch_shapes=[
            pltpu.VMEM((SECTIONS, 16, TILE, width), jnp.bfloat16),
            pltpu.VMEM((16, TILE, width), jnp.bfloat16),
            pltpu.VMEM((SECTIONS, SLOTS, TILE, TILE), jnp.bfloat16),
            pltpu.VMEM((REPS, weight.shape[0], weight.shape[1]), jnp.bfloat16),
            pltpu.VMEM((SECTIONS * SLOTS + 1, TILE, TILE), jnp.float32),
            pltpu.VMEM((REPS, height // REPS, width), jnp.bfloat16),
            pltpu.VMEM((REPS, height // REPS, width), jnp.bfloat16),
            pltpu.SMEM(tile_rows.shape, jnp.int32),
            pltpu.SMEM(tile_cols.shape, jnp.int32),
            pltpu.SMEM(tile_counts.shape, jnp.int32),
            pltpu.SMEM((SECTIONS * SLOTS,), jnp.int32),
            pltpu.SMEM((16,), jnp.int32),
            dma((6,)),
            dma((SECTIONS, 14)),
            dma((SECTIONS, 40)),
            dma((REPS,)),
            dma((REPS,)),
            dma((REPS,)),
            dma((REPS,)),
        ],
        compiler_params=pltpu.CompilerParams(
            collective_id=0, has_side_effects=True, vmem_limit_bytes=60 << 20
        ),
        cost_estimate=pl.CostEstimate(flops=1_610_612_736, bytes_accessed=8_000_000, transcendentals=0),
        name="layer",
    )(tile_rows, tile_cols, tile_counts, features.reshape(16, TILE, width), tile_values, weight)


def solution(mesh):
    return jax.shard_map(
        shards,
        mesh=mesh,
        in_specs=(
            P("rows", "rep"),
            P("rows", None, None),
            P("rows", None, None),
            P("rows", None),
            P("rows", None, None, None, None),
            P(None, "rep"),
        ),
        out_specs=P(("rows", "rep"), None),
        check_vma=False,
    )
```

time: 75.3 us -> 72.6 us (0.964)
  Pallas kernels: 73.2 us -> 71.7 us
  local copies, waits for them, and re-layouts: 1.87 us -> 0.8 us
    pallas_call x1, Pallas kernels: 73.2 us -> 71.7 us  [shards(): pl.pallas_call(kernel, out_shape=OUT((height // REPS, width * REPS), jnp....]
    unnamed x1, local copies, waits for them, and re-layouts: 1.87 us -> 0.8 us
where the time goes in v2:
time: 72.6 us; the launch traced here: 72.5 us
  Pallas kernels  71.7 us (99%)
  local copies, waits for them, and re-layouts  0.8 us (1%)
    pallas_call x1, Pallas kernels, shards(): pl.pallas_call(kernel, out_shape=OUT((height // REPS, width * REPS), jnp....  71.7 us

profile of v2, /device:TPU:1, one launch (start us, length us, event | category | flops | bytes accessed | tf_op | source)
XLA Modules:
  0.0 72.5 jit_solution(2922479676554989723)
XLA Ops:
  0.0 71.7 %layer.1 = bf16[256,1024]{1,0:T(8,128)(2,1)S(1)} custom-call(s32[1,4,16]{2,1,0:T(4,128)} %rows_hbm.1, s32[1,4,16]{2,1,0:T(4,128)} %cols_hbm.1, s32[1,4]{1,0:T(1,128)} %counts_hbm.1, bf16[16,128,128]{2,1,0:T(8,128)(2,1)} %bitcast.1, bf16[1,4,16,128,128]{4,3,2,1,0:T(8,128)(2,1)} %tiles_ref.1, bf16[1024,128]{1,0:T(8,128)(2,1)} %weight_ref.1), custom_call_target="tpu_custom_call" | custom-call | flops 1610612736 | bytes 8000000 | tf_op jit(solution)/shard_map/layer/pallas_call | solution.py:327
  71.7 0.8 %copy.8 = bf16[256,1024]{1,0:T(8,128)(2,1)} copy(bf16[256,1024]{1,0:T(8,128)(2,1)S(1)} %layer.1) | data formatting | bytes 1048576

commit v3 on v2

--- a/solution.py
+++ b/solution.py
@@ -109,6 +109,12 @@
         return pltpu.make_async_remote_copy(
             ref, ref, send_sem.at[section, send], recv_sem.at[section, recv], device_id=to, device_id_type=MESH)
 
+    def piece(section, group, b, h, send, recv, to):
+        ref = panel.at[section, 4 * group + b, pl.ds(h * (TILE // 2), TILE // 2)]
+        return pltpu.make_async_remote_copy(
+            ref, ref, send_sem.at[section, send + 40 * h], recv_sem.at[section, recv + 14 * h],
+            device_id=to, device_id_type=MESH)
+
     def gets(section):
         dz, _ = along(section)
         return jnp.logical_or(dz != 0, x != 0)
@@ -122,34 +128,37 @@
             @pl.when(x == 0)
             def _():
                 for b in (0, 3, 1, 2):
-                    for i, dx in enumerate((2, 1, 3)):
-                        act(copy(section, dx, b, 3 * b + i, b, at(0, dx)))
+                    for h in range(2):
+                        for i, dx in enumerate((2, 1, 3)):
+                            act(piece(section, dx, b, h, 3 * b + i, b, at(0, dx)))
 
             needs = {4: (0,), 3: (3, 1), 2: (2,)}
             for d in range(HOP, 0, -1):
-                if wait and d in needs:
-                    @pl.when(x != 0)
-                    def _():
-                        for b in needs[d]:
-                            copy(section, x, b, 0, b, at(0, 1)).wait_recv()
-
-                act(copy(section, x, d % 4, 10 + 2 * d, 0, at(d, 0)))
-                act(copy(section, x, -d % 4, 11 + 2 * d, 0, at(-d, 0)))
+                for h in range(2):
+                    if wait and d in needs:
+                        @pl.when(x != 0)
+                        def _():
+                            for b in needs[d]:
+                                piece(section, x, b, h, 0, b, at(0, 1)).wait_recv()
+
+                    act(piece(section, x, d % 4, h, 10 + 2 * d, 0, at(d, 0)))
+                    act(piece(section, x, -d % 4, h, 11 + 2 * d, 0, at(-d, 0)))
 
         own = z % 4
 
         @pl.when(jnp.logical_not(in_row))
         def _():
-            if wait:
-                copy(section, x, own, 0, 0, at(1, 0)).wait_recv()
-
-            @pl.when(dz <= HALF - HOP)
-            def _():
-                act(copy(section, x, own, 12, 0, at(HOP, 0)))
-
-            @pl.when(dz > HALF + HOP)
-            def _():
-                act(copy(section, x, own, 12, 0, at(-HOP, 0)))
+            for h in range(2):
+                if wait:
+                    piece(section, x, own, h, 0, 0, at(1, 0)).wait_recv()
+
+                @pl.when(dz <= HALF - HOP)
+                def _():
+                    act(piece(section, x, own, h, 12, 0, at(HOP, 0)))
+
+                @pl.when(dz > HALF + HOP)
+                def _():
+                    act(piece(section, x, own, h, 12, 0, at(-HOP, 0)))
 
         out = dz <= HALF
         far = jnp.where(out, dz, ZS - dz)
@@ -343,8 +352,8 @@
             pltpu.SMEM((SECTIONS * SLOTS,), jnp.int32),
             pltpu.SMEM((16,), jnp.int32),
             dma((6,)),
-            dma((SECTIONS, 14)),
-            dma((SECTIONS, 40)),
+            dma((SECTIONS, 18)),
+            dma((SECTIONS, 60)),
             dma((REPS,)),
             dma((REPS,)),
             dma((REPS,)),

time: 72.6 us -> 72.7 us (level)
  no operation moved by 1% of the time
where the time goes in v3:
time: 72.7 us; the launch traced here: 72.6 us
  Pallas kernels  71.8 us (99%)
  local copies, waits for them, and re-layouts  0.8 us (1%)
    pallas_call x1, Pallas kernels, shards(): pl.pallas_call(kernel, out_shape=OUT((height // REPS, width * REPS), jnp....  71.8 us

profile of v3, /device:TPU:1, one launch (start us, length us, event | category | flops | bytes accessed | tf_op | source)
XLA Modules:
  0.0 72.6 jit_solution(7098911437545423386)
XLA Ops:
  0.0 71.8 %layer.1 = bf16[256,1024]{1,0:T(8,128)(2,1)S(1)} custom-call(s32[1,4,16]{2,1,0:T(4,128)} %rows_hbm.1, s32[1,4,16]{2,1,0:T(4,128)} %cols_hbm.1, s32[1,4]{1,0:T(1,128)} %counts_hbm.1, bf16[16,128,128]{2,1,0:T(8,128)(2,1)} %bitcast.1, bf16[1,4,16,128,128]{4,3,2,1,0:T(8,128)(2,1)} %tiles_ref.1, bf16[1024,128]{1,0:T(8,128)(2,1)} %weight_ref.1), custom_call_target="tpu_custom_call" | custom-call | flops 1610612736 | bytes 8000000 | tf_op jit(solution)/shard_map/layer/pallas_call | solution.py:336
  71.8 0.8 %copy.8 = bf16[256,1024]{1,0:T(8,128)(2,1)} copy(bf16[256,1024]{1,0:T(8,128)(2,1)S(1)} %layer.1) | data formatting | bytes 1048576
